TPU v7x, 256 devices: a whole 4x4x8 slice. The times are simulated.
256 devices in a mesh: lat: 16 (over z_lo, y, core), lev: 4 (over x), ocn: 4 (over z_hi).
Axes of the slice: x: 4, y: 4, z: 8 (z_hi: 4, z_lo: 2; z = z_hi * 2 + z_lo), core: 2. Of those that a mesh axis runs over, the one named last changes fastest.
Arguments:
- atmos_fields: bfloat16 [2, 24, 2560, 5632], P(None, 'lev', ('lat', 'ocn')), may hold values from -6 to 6
- lat_points: int32 [2560], P(('lat', 'ocn')), may hold values from 20 to 5632, as said below
- wave_order: int32 [256], replicated, may hold values from 0 to 255, each once
- legendre: bfloat16 [256, 2560, 1536], P(('lat', 'ocn'), None, 'lev'), may hold values from -0.125 to 0.125
- column_weight: bfloat16 [2, 24], P(None, 'lev'), may hold values from -1.25 to 1.25
- block_remap: int32 [2560, 44], P(('lat', 'ocn'), 'lev'), may hold values from 0 to 17407, as said below
- ocean_temp: float32 [1024, 2176], P(('lat', 'ocn')), may hold values from -6 to 6
- ocean_salt: float32 [1024, 2176], P(('lat', 'ocn')), may hold values from -6 to 6
- sea_mask: int32 [1024, 17], P(('lat', 'ocn')), may hold values 0 or 1
Outputs:
- spectra: float32 [256, 96, 1536], P(('lat', 'ocn'), None, 'lev')
- temp_next: float32 [1024, 2176], P(('lat', 'ocn'))
- salt_next: float32 [1024, 2176], P(('lat', 'ocn'))
- surface_temp: float32 [2560, 5632], P(('lat', 'ocn'), 'lev')
Inputs may be any that keep to these rules, and one draw needn't show every extreme that they name: `lat_points`: a multiple of 4 for every latitude row. `wave_order`: each wavenumber appears once. `block_remap`: the blocks of latitude band g (rows g * 40 onward) name tiles of ocean sections g - 1, g or g + 1 only; section g holds tiles g * 16 * 17 onward, in row order.
All inputs are finite; a program needn't handle non-finite values. No bound on the sum of `sea_mask` on one device may be relied on, other than what follows from the above.
Results may differ from a plain program's by a relative error of at most 0.0037.
Values may be sent and summed in bfloat16 or wider, within the bound.
A program may use at most 128 MiB of HBM per device.

v0:
```python
import math
import jax
import jax.numpy as jnp
from jax import lax
from jax.sharding import PartitionSpec as P

FIELDS = 2
BLOCK = 128
FULL_TURN = 2.0 * math.pi
DIFFUSION = 0.2
COUPLING = 0.5


def with_halo(cells, sides, width):
    for axis, dim in sides:
        count = lax.axis_size(axis)
        ends = count - 1
        head = lax.slice_in_dim(cells, 0, width, axis=dim)
        tail = lax.slice_in_dim(cells, cells.shape[dim] - width, cells.shape[dim], axis=dim)
        cells = jnp.concatenate(
            [
                lax.ppermute(tail, axis, [(i, (i + 1) % count) for i in range(ends)]),
                cells,
                lax.ppermute(head, axis, [((i + 1) % count, i) for i in range(ends)]),
            ],
            axis=dim,
        )
    return cells


def fourier_table(wave_order, length):
    points = jnp.arange(length, dtype=jnp.int32)
    phase = wave_order[None, :] * points[:, None] % length
    angle = phase.astype(jnp.float32) * (FULL_TURN / length)
    table = jnp.concatenate([jnp.cos(angle), -jnp.sin(angle)], axis=1).astype(jnp.bfloat16)
    return (table, points)


def body(
    atmos_fields,
    lat_points,
    wave_order,
    legendre,
    column_weight,
    block_remap,
    ocean_temp,
    ocean_salt,
    sea_mask,
):
    nfields, lev_dev, lat_band, lon_count = atmos_fields.shape
    wave_count = wave_order.shape[0]
    table, points = fourier_table(wave_order, lon_count)
    point_mask = points[None, :] < lat_points[:, None]
    masked = jnp.where(point_mask[None, None], atmos_fields, jnp.zeros((), jnp.bfloat16))
    inverse_root = 1.0 / jnp.sqrt(lat_points.astype(jnp.float32))
    weights = jnp.where(
        2 * wave_order[None, :] < lat_points[:, None],
        inverse_root[:, None],
        jnp.zeros((), jnp.float32),
    )
    field_count = masked.shape[0]
    raw_sums = jnp.dot(masked.reshape(-1, lon_count), table, preferred_element_type=jnp.float32)
    raw_sums = raw_sums.reshape(field_count, lev_dev, lat_band, 2, wave_count)
    coeffs = (raw_sums * weights[None, None, :, None, :]).astype(jnp.bfloat16)
    regrouped = lax.all_to_all(
        coeffs.transpose(4, 1, 0, 3, 2).reshape(wave_count, lev_dev * field_count * 2, lat_band),
        ("lat", "ocn"),
        split_axis=0,
        concat_axis=2,
        tiled=True,
    )
    spectra = jnp.einsum(
        "srj,sjd->srd",
        lax.all_gather(regrouped, "lev", axis=1, tiled=True),
        legendre,
        preferred_element_type=jnp.float32,
    )
    ocean_rows, ocean_cols = ocean_temp.shape
    tile_count = ocean_rows * ocean_cols // BLOCK
    band_index = lax.axis_index(("lat", "ocn"))
    targets = block_remap.reshape(-1)
    local_slot = (targets // tile_count - band_index + 1) * tile_count + targets % tile_count
    partial_sum = jnp.einsum(
        "ql,qljk->qjk", column_weight, masked, preferred_element_type=jnp.float32
    )
    quarter = lon_count // lax.axis_size("lev")
    totals = lax.psum(partial_sum, "lev")
    own_flux = lax.dynamic_slice_in_dim(totals, lax.axis_index("lev") * quarter, quarter, 2)
    block_rows = (
        own_flux.reshape(FIELDS, lat_band, quarter // BLOCK, BLOCK)
        .transpose(1, 2, 0, 3)
        .reshape(-1, FIELDS * BLOCK)
    )
    outgoing = jax.ops.segment_sum(block_rows, local_slot, num_segments=3 * tile_count)
    widened = with_halo(outgoing, ((("lat", "ocn"), 0),), tile_count)
    arrived = (
        widened[:tile_count] + widened[2 * tile_count : 3 * tile_count] + widened[4 * tile_count :]
    )
    tile_sums = lax.psum(arrived, "lev")
    forcing = (
        tile_sums.reshape(ocean_rows, ocean_cols // BLOCK, FIELDS, BLOCK)
        .transpose(2, 0, 1, 3)
        .reshape(FIELDS, ocean_rows, ocean_cols)
    )
    sea_cells = (
        jnp.broadcast_to(sea_mask[:, :, None], (ocean_rows, ocean_cols // BLOCK, BLOCK))
        .reshape(ocean_rows, ocean_cols)
        .astype(jnp.float32)
    )
    ocean_state = jnp.stack([ocean_temp, ocean_salt])
    padded = with_halo(ocean_state, ((("lat", "ocn"), 1),), 1)
    laplace = (
        padded[:, 2:]
        + padded[:, :-2]
        + jnp.roll(ocean_state, 1, 2)
        + jnp.roll(ocean_state, -1, 2)
        - 4.0 * ocean_state
    )
    updated = ocean_state + DIFFUSION * laplace + COUPLING * sea_cells[None] * forcing
    temp_next = updated[0]
    salt_next = updated[1]
    returned = with_halo(temp_next, ((("lat", "ocn"), 0),), ocean_rows)
    tiles_near = returned.reshape(3 * tile_count, BLOCK)
    surface = jnp.take(tiles_near, local_slot, axis=0).reshape(lat_band, quarter)
    own_points = lax.axis_index("lev") * quarter + jnp.arange(quarter, dtype=jnp.int32)
    surface_temp = jnp.where(
        own_points[None, :] < lat_points[:, None], surface, jnp.zeros((), jnp.float32)
    )
    return (spectra, temp_next, salt_next, surface_temp)


def solution(mesh):
    placed = (
        P(None, "lev", ("lat", "ocn"), None),
        P(("lat", "ocn")),
        P(),
        P(("lat", "ocn"), None, "lev"),
        P(None, "lev"),
        P(("lat", "ocn"), "lev"),
        P(("lat", "ocn"), None),
        P(("lat", "ocn"), None),
        P(("lat", "ocn"), None),
    )
    return jax.shard_map(
        body,
        mesh=mesh,
        in_specs=placed,
        out_specs=(
            P(("lat", "ocn"), None, "lev"),
            P(("lat", "ocn"), None),
            P(("lat", "ocn"), None),
            P(("lat", "ocn"), "lev"),
        ),
        check_vma=False,
    )
```

profile of v0, /device:TPU:1, one launch (start us, length us, event | category | flops | bytes accessed | tf_op | source)
XLA Modules:
  0.0 199.3 jit_solution(3094316823144433169)
XLA Ops:
  8.1 3.6 %broadcast_select_fusion = bf16[2,6,40,5632]{3,2,1,0:T(8,128)(2,1)S(1)} fusion(bf16[2,6,40,5632]{3,2,1,0:T(8,128)(2,1)} %param.9, pred[40,5632]{1,0:T(8,128)(4,1)S(1)} %iota_compare_fusion), kind=kLoop, calls=%fused_computation.16 | loop fusion | flops 2703360 | bytes 11038720 | tf_op jit(solution)/shard_map/jit(_where)/select_n | solution.py:54
  11.7 2.4 %fusion = f32[2,1,40,5632]{3,1,2,0:T(1,128)S(1)} fusion(bf16[2,6,40,5632]{3,2,1,0:T(8,128)(2,1)S(1)} %broadcast_select_fusion, bf16[2,6,1,1]{1,0,2,3:T(2,128)(2,1)S(1)} %bitcast.59), kind=kOutput, calls=%fused_computation.3 | convolution fusion | flops 5406720 | bytes 7208984 | tf_op jit(solution)/shard_map/ql,qljk->qjk/dot_general | solution.py:83
  15.6 25.0 %cosine_convert_fusion = (bf16[5632,256]{0,1:T(8,128)(2,1)S(1)}, bf16[5632,256]{0,1:T(8,128)(2,1)S(1)}) fusion(s32[256]{0:T(256)S(1)} %copy-done.8), kind=kLoop, calls=%fused_computation.9 | loop fusion | flops 17301504 | bytes 5768192 | tf_op jit(solution)/shard_map/convert
  40.7 2.9 %pad_maximum_fusion = bf16[5632,512]{0,1:T(8,128)(2,1)} fusion(bf16[5632,256]{0,1:T(8,128)(2,1)S(1)} %get-tuple-element.21, bf16[5632,256]{0,1:T(8,128)(2,1)S(1)} %get-tuple-element.20), kind=kLoop, calls=%fused_computation.7 | loop fusion | flops 11534336 | bytes 11534336 | tf_op jit(solution)/shard_map/concatenate | solution.py:35
  43.6 5.7 %fusion.15 = bf16[256,6,2,2,40]{0,4,3,1,2:T(8,128)(2,1)S(1)} fusion(bf16[2,256,5632,1,1]{2,1,0,4,3:T(8,128)(2,1)} %bitcast.64, bf16[2,6,40,5632]{3,2,1,0:T(8,128)(2,1)S(1)} %bitcast.61, f32[256,40]{0,1:T(8,128)S(1)} %compare_select_fusion), kind=kOutput, calls=%fused_computation.20 | convolution fusion | flops 2768732160 | bytes 11706368 | tf_op jit(solution)/shard_map/dot_general | solution.py:62
  50.3 3.4 %reshape.235 = bf16[64,2,1920]{2,1,0:T(2,128)(2,1)} reshape(bf16[256,24,40]{2,1,0:T(8,128)(2,1)S(1)} %copy.32) | data formatting | bytes 983040
  53.7 13.3 %all-to-all-start = ((bf16[64,2,1920]{2,1,0:T(2,128)(2,1)}), bf16[64,2,1920]{2,1,0:T(2,128)(2,1)S(1)}, u32[]{:S(2)}, u32[]{:S(2)}) async-start(bf16[64,2,1920]{2,1,0:T(2,128)(2,1)} %reshape.235), calls=%async_computation | async-start | bytes 983040 | tf_op jit(solution)/shard_map/all_to_all | solution.py:65
  67.9 10.6 %all-reduce.3.cloned.1.call-done = f32[2,40,5632]{2,1,0:T(8,128)} async-done(((f32[2,40,5632]{2,1,0:T(8,128)}), f32[2,40,5632]{2,1,0:T(8,128)}) %all-reduce.3.cloned.1.call-update) | async-done | bytes 1802256 | tf_op jit(solution)/shard_map/psum | solution.py:87
  80.0 3.1 %scatter_custom_fusion = f32[816,256]{1,0:T(8,128)S(1)} fusion(s32[440]{0:T(512)S(1)} %bitcast.81, f32[55,8,2,128]{3,2,1,0:T(2,128)S(1)} %bitcast.75, f32[]{:T(128)} %constant.40.clone.1), kind=kCustom, calls=%fused_computation.35 | custom fusion | flops 112640 | bytes 1286148 | tf_op jit(solution)/shard_map/scatter-add | solution.py:94
  83.2 6.3 %collective-permute-start.3 = (f32[272,256]{1,0:T(8,128)S(1)}, f32[272,256]{1,0:T(8,128)S(1)}, u32[]{:S(2)}, u32[]{:S(2)}) collective-permute-start(f32[272,256]{1,0:T(8,128)S(1)} %get-tuple-element.9), channel_id=1, source_target_pairs={{1,0},{2,1},{3,2},{16,3},{17,16},{18,17},{19,18},{32,19},{33,32},{... | collective-permute-start | bytes 835592 | tf_op jit(solution)/shard_map/ppermute | solution.py:24
  89.5 1.9 collective-permute-start.2
  91.4 8.1 %collective-permute-done.3 = f32[272,256]{1,0:T(8,128)S(1)} collective-permute-done((f32[272,256]{1,0:T(8,128)S(1)}, f32[272,256]{1,0:T(8,128)S(1)}, u32[]{:S(2)}, u32[]{:S(2)}) %collective-permute-start.3) | collective-permute-done | bytes 278560 | tf_op jit(solution)/shard_map/ppermute | solution.py:24
  99.6 8.0 %collective-permute-done.2 = f32[272,256]{1,0:T(8,128)S(1)} collective-permute-done((f32[272,256]{1,0:T(8,128)S(1)}, f32[272,256]{1,0:T(8,128)S(1)}, u32[]{:S(2)}, u32[]{:S(2)}) %collective-permute-start.2) | collective-permute-done | bytes 278560 | tf_op jit(solution)/shard_map/ppermute | solution.py:22
  108.7 1.9 collective-permute-start.1
  110.7 5.8 %collective-permute-start = (f32[2,1,2176]{2,1,0:T(1,128)S(1)}, f32[2,1,2176]{2,1,0:T(1,128)S(1)}, u32[]{:S(2)}, u32[]{:S(2)}) collective-permute-start(f32[2,1,2176]{2,1,0:T(1,128)S(1)} %get-tuple-element.16), channel_id=1, source_target_pairs={{1,0},{2,1},{3,2},{16,3},{17,16},{18,17},{19,18},{32,19},{33,32},{... | collective-permute-start | bytes 52232 | tf_op jit(solution)/shard_map/ppermute | solution.py:24
  116.4 2.5 %reshape.236 = bf16[256,24,40]{2,1,0:T(8,128)(2,1)S(1)} reshape(bf16[64,2,1920]{2,1,0:T(2,128)(2,1)S(1)} %all-to-all-done) | data formatting | bytes 983040
  119.6 3.9 %all_to_all.16 = bf16[4,24,2560]{2,1,0:T(8,128)(2,1)} reshape(bf16[4,24,64,40]{3,2,1,0:T(8,128)(2,1)S(1)} %copy.33) | data formatting | bytes 983040 | tf_op jit(solution)/shard_map/all_to_all | solution.py:65
  123.9 25.7 %all-reduce.5.cloned.1.call-done = f32[2,16,2176]{2,1,0:T(8,128)} async-done(((f32[2,16,2176]{2,1,0:T(8,128)}), f32[2,16,2176]{2,1,0:T(8,128)}) %all-reduce.5.cloned.1.call-update) | async-done | bytes 278544 | tf_op jit(solution)/shard_map/psum | solution.py:99
  151.4 8.4 %collective-permute-start.5 = (f32[16,2176]{1,0:T(8,128)S(1)}, f32[16,2176]{1,0:T(8,128)S(1)}, u32[]{:S(2)}, u32[]{:S(2)}) collective-permute-start(f32[16,2176]{1,0:T(8,128)S(1)} %get-tuple-element.11), channel_id=1, source_target_pairs={{1,0},{2,1},{3,2},{16,3},{17,16},{18,17},{19,18},{32,19},{33,32},{... | collective-permute-start | bytes 417800 | tf_op jit(solution)/shard_map/ppermute | solution.py:24
  159.8 1.9 collective-permute-start.4
  161.9 2.9 %collective-permute-done.5 = f32[16,2176]{1,0:T(8,128)S(1)} collective-permute-done((f32[16,2176]{1,0:T(8,128)S(1)}, f32[16,2176]{1,0:T(8,128)S(1)}, u32[]{:S(2)}, u32[]{:S(2)}) %collective-permute-start.5) | collective-permute-done | bytes 139296 | tf_op jit(solution)/shard_map/ppermute | solution.py:24
  164.8 5.0 %collective-permute-done.4 = f32[16,2176]{1,0:T(8,128)S(1)} collective-permute-done((f32[16,2176]{1,0:T(8,128)S(1)}, f32[16,2176]{1,0:T(8,128)S(1)}, u32[]{:S(2)}, u32[]{:S(2)}) %collective-permute-start.4) | collective-permute-done | bytes 139296 | tf_op jit(solution)/shard_map/ppermute | solution.py:22
  172.0 14.7 %all-gather.2.cloned.1.call-done = bf16[4,96,2560]{2,1,0:T(8,128)(2,1)} async-done(((bf16[4,24,2560]{2,1,0:T(8,128)(2,1)}), bf16[4,96,2560]{2,1,0:T(8,128)(2,1)}) %all-gather.2.cloned.1.call-update) | async-done | bytes 1966096 | tf_op jit(solution)/shard_map/all_gather | solution.py:74
  186.7 6.1 %fusion.44 = f32[4,96,384]{2,1,0:T(8,128)} fusion(bf16[4,96,2560]{2,1,0:T(8,128)(2,1)} %all-gather.2.cloned.1.call-done, bf16[4,2560,384]{2,1,0:T(8,128)(2,1)} %param.12), kind=kOutput, calls=%fused_computation.87 | convolution fusion | flops 754974720 | bytes 10420224 | tf_op jit(solution)/shard_map/srj,sjd->srd/dot_general | solution.py:72
  (74 shorter events, 11.8 us)
Async XLA Ops:
  7.2 4.5 %copy-start = (bf16[2,6]{1,0:T(2,128)(2,1)S(1)}, bf16[2,6]{1,0:T(2,128)(2,1)}, u32[]{:S(2)}) copy-start(bf16[2,6]{1,0:T(2,128)(2,1)} %param.13) | copy-start | bytes 76
  7.2 71.3 %all-reduce.3.cloned.1.call-start = ((), (), s32[]{:S(2)}) async-start(), calls=%async_computation.2 | async-start | bytes 3604480 | tf_op jit(solution)/shard_map/psum | solution.py:87
  11.7 3.8 %copy-start.1 = (bf16[2,6,40,5632]{3,2,1,0:T(8,128)(2,1)}, bf16[2,6,40,5632]{3,2,1,0:T(8,128)(2,1)S(1)}, u32[]{:S(2)}) copy-start(bf16[2,6,40,5632]{3,2,1,0:T(8,128)(2,1)S(1)} %broadcast_select_fusion) | copy-start | bytes 16220164
  11.7 3.8 %copy-start.7 = (s32[40]{0:T(128)S(1)}, s32[40]{0:T(128)}, u32[]{:S(2)}) copy-start(s32[40]{0:T(128)} %param.10) | copy-start | bytes 484
  11.7 3.8 %copy-start.8 = (s32[256]{0:T(256)S(1)}, s32[256]{0:T(256)}, u32[]{:S(2)}) copy-start(s32[256]{0:T(256)} %param.11) | copy-start | bytes 3076
  15.6 28.0 %slice-start = ((s8[5406720]{0:T(1024)(128)(4,1)}), s8[4194304]{0:T(1024)(128)(4,1)S(1)}, s32[]{:S(2)}) async-start(s8[5406720]{0:T(1024)(128)(4,1)} %bitcast.60), calls=%async_computation.4 | async-start | bytes 8388608
  40.6 3.0 %slice-start.1 = ((s8[5406720]{0:T(1024)(128)(4,1)}), s8[1212416]{0:T(1024)(128)(4,1)S(1)}, s32[]{:S(2)}) async-start(s8[5406720]{0:T(1024)(128)(4,1)} %bitcast.60), calls=%async_computation.5 | async-start | bytes 2424832
  49.3 17.8 %copy-start.5 = (s32[40,11]{0,1:T(8,128)S(1)}, s32[40,11]{0,1:T(8,128)}, u32[]{:S(2)}) copy-start(s32[40,11]{0,1:T(8,128)} %param.14) | copy-start | bytes 5284
  53.7 54.9 %copy-start.2 = (f32[16,2176]{1,0:T(8,128)S(1)}, f32[16,2176]{1,0:T(8,128)}, u32[]{:S(2)}) copy-start(f32[16,2176]{1,0:T(8,128)} %param.15) | copy-start | bytes 417796
  53.7 54.9 %copy-start.3 = (f32[16,2176]{1,0:T(8,128)S(1)}, f32[16,2176]{1,0:T(8,128)}, u32[]{:S(2)}) copy-start(f32[16,2176]{1,0:T(8,128)} %param.16) | copy-start | bytes 417796
  53.7 62.7 %all-to-all-start = ((bf16[64,2,1920]{2,1,0:T(2,128)(2,1)}), bf16[64,2,1920]{2,1,0:T(2,128)(2,1)S(1)}, u32[]{:S(2)}, u32[]{:S(2)}) async-start(bf16[64,2,1920]{2,1,0:T(2,128)(2,1)} %reshape.235), calls=%async_computation | async-start | bytes 983040 | tf_op jit(solution)/shard_map/all_to_all | solution.py:65
  67.1 82.5 %all-reduce.5.cloned.1.call-start = ((), (), s32[]{:S(2)}) async-start(), calls=%async_computation.3 | async-start | bytes 557056 | tf_op jit(solution)/shard_map/psum | solution.py:99
  83.2 16.4 %collective-permute-start.3 = (f32[272,256]{1,0:T(8,128)S(1)}, f32[272,256]{1,0:T(8,128)S(1)}, u32[]{:S(2)}, u32[]{:S(2)}) collective-permute-start(f32[272,256]{1,0:T(8,128)S(1)} %get-tuple-element.9), channel_id=1, source_target_pairs={{1,0},{2,1},{3,2},{16,3},{17,16},{18,17},{19,18},{32,19},{33,32},{... | collective-permute-start | bytes 835592 | tf_op jit(solution)/shard_map/ppermute | solution.py:24
  89.5 18.1 %collective-permute-start.2 = (f32[272,256]{1,0:T(8,128)S(1)}, f32[272,256]{1,0:T(8,128)S(1)}, u32[]{:S(2)}, u32[]{:S(2)}) collective-permute-start(f32[272,256]{1,0:T(8,128)S(1)} %get-tuple-element.8), channel_id=1, source_target_pairs={{0,1},{1,2},{2,3},{3,16},{16,17},{17,18},{18,19},{19,32},{32,33},{... | collective-permute-start | bytes 835592 | tf_op jit(solution)/shard_map/ppermute | solution.py:22
  107.6 15.8 %copy-start.6 = (s32[16,17]{1,0:T(8,128)S(1)}, s32[16,17]{1,0:T(8,128)}, u32[]{:S(2)}) copy-start(s32[16,17]{1,0:T(8,128)} %param.17) | copy-start | bytes 3268
  108.6 78.1 %all-gather.2.cloned.1.call-start = ((), (), s32[]{:S(2)}) async-start(), calls=%async_computation.1 | async-start | bytes 2457600 | tf_op jit(solution)/shard_map/all_gather | solution.py:74
  108.7 15.1 %collective-permute-start.1 = (f32[2,1,2176]{2,1,0:T(1,128)S(1)}, f32[2,1,2176]{2,1,0:T(1,128)S(1)}, u32[]{:S(2)}, u32[]{:S(2)}) collective-permute-start(f32[2,1,2176]{2,1,0:T(1,128)S(1)} %get-tuple-element.17), channel_id=1, source_target_pairs={{0,1},{1,2},{2,3},{3,16},{16,17},{17,18},{18,19},{19,32},{32,33},{... | collective-permute-start | bytes 52232 | tf_op jit(solution)/shard_map/ppermute | solution.py:22
  110.7 13.2 %collective-permute-start = (f32[2,1,2176]{2,1,0:T(1,128)S(1)}, f32[2,1,2176]{2,1,0:T(1,128)S(1)}, u32[]{:S(2)}, u32[]{:S(2)}) collective-permute-start(f32[2,1,2176]{2,1,0:T(1,128)S(1)} %get-tuple-element.16), channel_id=1, source_target_pairs={{1,0},{2,1},{3,2},{16,3},{17,16},{18,17},{19,18},{32,19},{33,32},{... | collective-permute-start | bytes 52232 | tf_op jit(solution)/shard_map/ppermute | solution.py:24
  151.4 41.4 %copy-start.4 = (f32[16,2176]{1,0:T(8,128)}, f32[16,2176]{1,0:T(8,128)S(1)}, u32[]{:S(2)}) copy-start(f32[16,2176]{1,0:T(8,128)S(1)} %get-tuple-element.11) | copy-start | bytes 417796
  151.4 13.4 %collective-permute-start.5 = (f32[16,2176]{1,0:T(8,128)S(1)}, f32[16,2176]{1,0:T(8,128)S(1)}, u32[]{:S(2)}, u32[]{:S(2)}) collective-permute-start(f32[16,2176]{1,0:T(8,128)S(1)} %get-tuple-element.11), channel_id=1, source_target_pairs={{1,0},{2,1},{3,2},{16,3},{17,16},{18,17},{19,18},{32,19},{33,32},{... | collective-permute-start | bytes 417800 | tf_op jit(solution)/shard_map/ppermute | solution.py:24
  159.8 10.0 %collective-permute-start.4 = (f32[16,2176]{1,0:T(8,128)S(1)}, f32[16,2176]{1,0:T(8,128)S(1)}, u32[]{:S(2)}, u32[]{:S(2)}) collective-permute-start(f32[16,2176]{1,0:T(8,128)S(1)} %get-tuple-element.11), channel_id=1, source_target_pairs={{0,1},{1,2},{2,3},{3,16},{16,17},{17,18},{18,19},{19,32},{32,33},{... | collective-permute-start | bytes 417800 | tf_op jit(solution)/shard_map/ppermute | solution.py:22
Sparse Core Ops, SparseCore 0:
  15.7 62.7 all-reduce.2
  108.7 40.7 all-reduce.4
  152.1 34.6 all-gather.1
where the time goes:
time: 200 us; the launch traced here: 199 us
  waiting for transfers between devices  75.1 us (38%)
  starting transfers between devices  39.7 us (20%)
  other arithmetic  37.9 us (19%)
  local copies, waits for them, and re-layouts  18.2 us (9%)
  matrix products  14.2 us (7%)
  between operations  14.2 us (7%)
    psum x1, waiting for transfers between devices, body(): tile_sums = lax.psum(arrived, 'lev')  25.7 us
    another operation x1, other arithmetic  25 us
    ppermute x3, starting transfers between devices, with_halo(): lax.ppermute(head, axis, [((i + 1) % count, i) for i in range(ends)])  20.5 us
    all_gather x1, waiting for transfers between devices, body(): lax.all_gather(regrouped, 'lev', axis=1, tiled=True)  14.7 us
    all_to_all x1, starting transfers between devices, body(): lax.all_to_all(coeffs.transpose(4, 1, 0, 3, 2).reshape(wave_count, lev_de...  13.3 us
    ppermute x3, waiting for transfers between devices, with_halo(): lax.ppermute(tail, axis, [(i, (i + 1) % count) for i in range(ends)])  13 us
    ppermute x3, waiting for transfers between devices, with_halo(): lax.ppermute(head, axis, [((i + 1) % count, i) for i in range(ends)])  11.1 us
    psum x1, waiting for transfers between devices, body(): totals = lax.psum(partial_sum, 'lev')  10.6 us
  transfers between devices with their start and end apart: 10, of which 7 were waited for; matrix products, arithmetic and copies ran while one was open for 26% of the time, Pallas kernels for 0%

commit v1 on v0

--- a/solution.py
+++ b/solution.py
@@ -9,6 +9,13 @@
 FULL_TURN = 2.0 * math.pi
 DIFFUSION = 0.2
 COUPLING = 0.5
+
+
+def swapped_in(x, axis, dim):
+    size = lax.axis_size(axis)
+    blocks = jnp.stack([x for _ in range(size)])
+    blocks = lax.all_to_all(blocks, axis, split_axis=0, concat_axis=0)
+    return jnp.concatenate(blocks, axis=dim)
 
 
 def with_halo(cells, sides, width):
@@ -71,7 +78,7 @@
     )
     spectra = jnp.einsum(
         "srj,sjd->srd",
-        lax.all_gather(regrouped, "lev", axis=1, tiled=True),
+        swapped_in(regrouped, "lev", 1),
         legendre,
         preferred_element_type=jnp.float32,
     )

time: 200 us -> 183 us (0.915); the launches traced: 199 us -> 180 us
  waiting for transfers between devices: 75.1 us -> 50.7 us
  starting transfers between devices: 39.7 us -> 43.1 us
    all_gather x1 -> x0, waiting for transfers between devices: 14.7 us -> none  [body(): lax.all_gather(regrouped, 'lev', axis=1, tiled=True)]
    psum x1, waiting for transfers between devices: 10.6 us -> 2.4 us  [body(): totals = lax.psum(partial_sum, 'lev')]
    psum x1, waiting for transfers between devices: 25.7 us -> 30.3 us  [body(): tile_sums = lax.psum(arrived, 'lev')]
    another operation x0 -> x2, local copies, waits for them, and re-layouts: none -> 4.52 us  [swapped_in(): blocks = jnp.stack([x for _ in range(size)])]
    all_to_all x2 -> x1, local copies, waits for them, and re-layouts: 4.47 us -> 0.61 us  [body(): lax.all_to_all(coeffs.transpose(4, 1, 0, 3, 2).reshape(wave_count, lev_de...]
    ppermute x3, waiting for transfers between devices: 11.1 us -> 7.27 us  [with_halo(): lax.ppermute(head, axis, [((i + 1) % count, i) for i in range(ends)])]
    all_to_all x0 -> x1, starting transfers between devices: none -> 3.6 us  [swapped_in(): blocks = lax.all_to_all(blocks, axis, split_axis=0, concat_axis=0)]
    ppermute x3, waiting for transfers between devices: 13 us -> 10.6 us  [with_halo(): lax.ppermute(tail, axis, [(i, (i + 1) % count) for i in range(ends)])]
  transfers between devices with their start and end apart: 10 -> 10, of which waited for: 7 -> 5; matrix products, arithmetic and copies ran while one was open for 26% -> 34% of each run, Pallas kernels for 0% -> 0%
where the time goes in v1:
time: 183 us; the launch traced here: 180 us
  waiting for transfers between devices  50.7 us (28%)
  starting transfers between devices  43.1 us (24%)
  other arithmetic  39.4 us (22%)
  local copies, waits for them, and re-layouts  19 us (10%)
  between operations  14.5 us (8%)
  matrix products  13.6 us (7%)
    psum x1, waiting for transfers between devices, body(): tile_sums = lax.psum(arrived, 'lev')  30.3 us
    another operation x1, other arithmetic  25 us
    ppermute x3, starting transfers between devices, with_halo(): lax.ppermute(head, axis, [((i + 1) % count, i) for i in range(ends)])  18.2 us
    all_to_all x1, starting transfers between devices, body(): lax.all_to_all(coeffs.transpose(4, 1, 0, 3, 2).reshape(wave_count, lev_de...  13.2 us
    ppermute x3, waiting for transfers between devices, with_halo(): lax.ppermute(tail, axis, [(i, (i + 1) % count) for i in range(ends)])  10.6 us
    ppermute x3, starting transfers between devices, with_halo(): lax.ppermute(tail, axis, [(i, (i + 1) % count) for i in range(ends)])  8.02 us
    ppermute x3, waiting for transfers between devices, with_halo(): lax.ppermute(head, axis, [((i + 1) % count, i) for i in range(ends)])  7.27 us
    unnamed x25, local copies, waits for them, and re-layouts  6.01 us
  transfers between devices with their start and end apart: 10, of which 5 were waited for; matrix products, arithmetic and copies ran while one was open for 34% of the time, Pallas kernels for 0%

profile of v1, /device:TPU:1, one launch (start us, length us, event | category | flops | bytes accessed | tf_op | source)
XLA Modules:
  0.0 180.3 jit_solution(8099330431604696891)
XLA Ops:
  8.1 3.6 %broadcast_select_fusion = bf16[2,6,40,5632]{3,2,1,0:T(8,128)(2,1)S(1)} fusion(bf16[2,6,40,5632]{3,2,1,0:T(8,128)(2,1)} %param.9, pred[40,5632]{1,0:T(8,128)(4,1)S(1)} %iota_compare_fusion), kind=kLoop, calls=%fused_computation.16 | loop fusion | flops 2703360 | bytes 11038720 | tf_op jit(solution)/shard_map/jit(_where)/select_n | solution.py:61
  11.7 2.4 %fusion = f32[2,1,40,5632]{3,1,2,0:T(1,128)S(1)} fusion(bf16[2,6,40,5632]{3,2,1,0:T(8,128)(2,1)S(1)} %broadcast_select_fusion, bf16[2,6,1,1]{1,0,2,3:T(2,128)(2,1)S(1)} %bitcast.61), kind=kOutput, calls=%fused_computation.3 | convolution fusion | flops 5406720 | bytes 7208984 | tf_op jit(solution)/shard_map/ql,qljk->qjk/dot_general | solution.py:90
  15.6 25.0 %cosine_convert_fusion = (bf16[5632,256]{0,1:T(8,128)(2,1)S(1)}, bf16[5632,256]{0,1:T(8,128)(2,1)S(1)}) fusion(s32[256]{0:T(256)S(1)} %copy-done.8), kind=kLoop, calls=%fused_computation.9 | loop fusion | flops 17301504 | bytes 5768192 | tf_op jit(solution)/shard_map/convert
  40.6 2.9 %pad_maximum_fusion = bf16[5632,512]{0,1:T(8,128)(2,1)} fusion(bf16[5632,256]{0,1:T(8,128)(2,1)S(1)} %get-tuple-element.21, bf16[5632,256]{0,1:T(8,128)(2,1)S(1)} %get-tuple-element.20), kind=kLoop, calls=%fused_computation.7 | loop fusion | flops 11534336 | bytes 11534336 | tf_op jit(solution)/shard_map/concatenate | solution.py:42
  43.6 5.7 %fusion.15 = bf16[256,6,2,2,40]{0,4,3,1,2:T(8,128)(2,1)S(1)} fusion(bf16[2,256,5632,1,1]{2,1,0,4,3:T(8,128)(2,1)} %bitcast.68, bf16[2,6,40,5632]{3,2,1,0:T(8,128)(2,1)S(1)} %bitcast.63, f32[256,40]{0,1:T(8,128)S(1)} %compare_select_fusion), kind=kOutput, calls=%fused_computation.20 | convolution fusion | flops 2768732160 | bytes 11706368 | tf_op jit(solution)/shard_map/dot_general | solution.py:69
  50.4 3.4 %reshape.246 = bf16[64,2,1920]{2,1,0:T(2,128)(2,1)} reshape(bf16[256,24,40]{2,1,0:T(8,128)(2,1)S(1)} %copy.32) | data formatting | bytes 983040
  53.8 13.2 %all-to-all-start = ((bf16[64,2,1920]{2,1,0:T(2,128)(2,1)}), bf16[64,2,1920]{2,1,0:T(2,128)(2,1)S(1)}, u32[]{:S(2)}, u32[]{:S(2)}) async-start(bf16[64,2,1920]{2,1,0:T(2,128)(2,1)} %reshape.246), calls=%async_computation | async-start | bytes 983040 | tf_op jit(solution)/shard_map/all_to_all | solution.py:72
  67.7 4.2 %collective-permute-start.1 = (f32[2,1,2176]{2,1,0:T(1,128)}, f32[2,1,2176]{2,1,0:T(1,128)S(1)}, u32[]{:S(2)}, u32[]{:S(2)}) collective-permute-start(f32[2,1,2176]{2,1,0:T(1,128)} %get-tuple-element.17), channel_id=1, source_target_pairs={{0,1},{1,2},{2,3},{3,16},{16,17},{17,18},{18,19},{19,32},{32,33},{... | collective-permute-start | bytes 52232 | tf_op jit(solution)/shard_map/ppermute | solution.py:29
  71.9 3.5 %collective-permute-start = (f32[2,1,2176]{2,1,0:T(1,128)S(1)}, f32[2,1,2176]{2,1,0:T(1,128)S(1)}, u32[]{:S(2)}, u32[]{:S(2)}) collective-permute-start(f32[2,1,2176]{2,1,0:T(1,128)S(1)} %get-tuple-element.16), channel_id=1, source_target_pairs={{1,0},{2,1},{3,2},{16,3},{17,16},{18,17},{19,18},{32,19},{33,32},{... | collective-permute-start | bytes 52232 | tf_op jit(solution)/shard_map/ppermute | solution.py:31
  76.1 2.4 %all-reduce.3.cloned.1.call-done = f32[2,40,5632]{2,1,0:T(8,128)} async-done(((f32[2,40,5632]{2,1,0:T(8,128)}), f32[2,40,5632]{2,1,0:T(8,128)}) %all-reduce.3.cloned.1.call-update) | async-done | bytes 1802256 | tf_op jit(solution)/shard_map/psum | solution.py:94
  80.0 3.1 %scatter_custom_fusion = f32[816,256]{1,0:T(8,128)S(1)} fusion(s32[440]{0:T(512)S(1)} %bitcast.85, f32[55,8,2,128]{3,2,1,0:T(2,128)S(1)} %bitcast.79, f32[]{:T(128)} %constant.40.clone.1), kind=kCustom, calls=%fused_computation.35 | custom fusion | flops 112640 | bytes 1286148 | tf_op jit(solution)/shard_map/scatter-add | solution.py:101
  83.2 6.3 %collective-permute-start.3 = (f32[272,256]{1,0:T(8,128)S(1)}, f32[272,256]{1,0:T(8,128)S(1)}, u32[]{:S(2)}, u32[]{:S(2)}) collective-permute-start(f32[272,256]{1,0:T(8,128)S(1)} %get-tuple-element.9), channel_id=1, source_target_pairs={{1,0},{2,1},{3,2},{16,3},{17,16},{18,17},{19,18},{32,19},{33,32},{... | collective-permute-start | bytes 835592 | tf_op jit(solution)/shard_map/ppermute | solution.py:31
  89.5 1.9 %collective-permute-start.2 = (f32[272,256]{1,0:T(8,128)S(1)}, f32[272,256]{1,0:T(8,128)S(1)}, u32[]{:S(2)}, u32[]{:S(2)}) collective-permute-start(f32[272,256]{1,0:T(8,128)S(1)} %get-tuple-element.8), channel_id=1, source_target_pairs={{0,1},{1,2},{2,3},{3,16},{16,17},{17,18},{18,19},{19,32},{32,33},{... | collective-permute-start | bytes 835592 | tf_op jit(solution)/shard_map/ppermute | solution.py:29
  92.3 7.3 %collective-permute-done.3 = f32[272,256]{1,0:T(8,128)S(1)} collective-permute-done((f32[272,256]{1,0:T(8,128)S(1)}, f32[272,256]{1,0:T(8,128)S(1)}, u32[]{:S(2)}, u32[]{:S(2)}) %collective-permute-start.3) | collective-permute-done | bytes 278560 | tf_op jit(solution)/shard_map/ppermute | solution.py:31
  99.6 8.0 %collective-permute-done.2 = f32[272,256]{1,0:T(8,128)S(1)} collective-permute-done((f32[272,256]{1,0:T(8,128)S(1)}, f32[272,256]{1,0:T(8,128)S(1)}, u32[]{:S(2)}, u32[]{:S(2)}) %collective-permute-start.2) | collective-permute-done | bytes 278560 | tf_op jit(solution)/shard_map/ppermute | solution.py:29
  108.7 2.5 %reshape.247 = bf16[256,24,40]{2,1,0:T(8,128)(2,1)S(1)} reshape(bf16[64,2,1920]{2,1,0:T(2,128)(2,1)S(1)} %all-to-all-done) | data formatting | bytes 983040
  111.8 3.1 %stack.18 = bf16[4,24,2560]{2,1,0:T(8,128)(2,1)S(1)} reshape(bf16[4,24,64,40]{3,2,1,0:T(8,128)(2,1)S(1)} %copy.33) | data formatting | bytes 983040 | tf_op jit(solution)/shard_map/stack | solution.py:16
  114.9 1.4 stack.19
  116.4 3.6 %all-to-all-start.1 = ((bf16[4,4,24,2560]{3,2,1,0:T(8,128)(2,1)}), bf16[4,4,24,2560]{3,2,1,0:T(8,128)(2,1)S(1)}, u32[]{:S(2)}, u32[]{:S(2)}) async-start(bf16[4,4,24,2560]{3,2,1,0:T(8,128)(2,1)} %stack.19), calls=%async_computation.1 | async-start | bytes 3932160 | tf_op jit(solution)/shard_map/all_to_all | solution.py:17
  120.3 30.3 %all-reduce.5.cloned.1.call-done = f32[2,16,2176]{2,1,0:T(8,128)} async-done(((f32[2,16,2176]{2,1,0:T(8,128)}), f32[2,16,2176]{2,1,0:T(8,128)}) %all-reduce.5.cloned.1.call-update) | async-done | bytes 278544 | tf_op jit(solution)/shard_map/psum | solution.py:106
  152.6 8.4 %collective-permute-start.5 = (f32[16,2176]{1,0:T(8,128)S(1)}, f32[16,2176]{1,0:T(8,128)S(1)}, u32[]{:S(2)}, u32[]{:S(2)}) collective-permute-start(f32[16,2176]{1,0:T(8,128)S(1)} %get-tuple-element.11), channel_id=1, source_target_pairs={{1,0},{2,1},{3,2},{16,3},{17,16},{18,17},{19,18},{32,19},{33,32},{... | collective-permute-start | bytes 417800 | tf_op jit(solution)/shard_map/ppermute | solution.py:31
  161.0 1.9 %collective-permute-start.4 = (f32[16,2176]{1,0:T(8,128)S(1)}, f32[16,2176]{1,0:T(8,128)S(1)}, u32[]{:S(2)}, u32[]{:S(2)}) collective-permute-start(f32[16,2176]{1,0:T(8,128)S(1)} %get-tuple-element.11), channel_id=1, source_target_pairs={{0,1},{1,2},{2,3},{3,16},{16,17},{17,18},{18,19},{19,32},{32,33},{... | collective-permute-start | bytes 417800 | tf_op jit(solution)/shard_map/ppermute | solution.py:29
  163.1 5.5 %fusion.44 = f32[4,96,384]{2,1,0:T(8,128)} fusion(bf16[4,96,2560]{2,1,0:T(8,128)(2,1)S(1)} %bitcast.64, bf16[4,2560,384]{2,1,0:T(8,128)(2,1)} %param.12), kind=kOutput, calls=%fused_computation.87 | convolution fusion | flops 754974720 | bytes 10420224 | tf_op jit(solution)/shard_map/srj,sjd->srd/dot_general | solution.py:79
  168.6 2.7 %collective-permute-done.4 = f32[16,2176]{1,0:T(8,128)S(1)} collective-permute-done((f32[16,2176]{1,0:T(8,128)S(1)}, f32[16,2176]{1,0:T(8,128)S(1)}, u32[]{:S(2)}, u32[]{:S(2)}) %collective-permute-start.4) | collective-permute-done | bytes 139296 | tf_op jit(solution)/shard_map/ppermute | solution.py:29
  (75 shorter events, 13.5 us)
Async XLA Ops:
  7.2 4.5 %copy-start = (bf16[2,6]{1,0:T(2,128)(2,1)S(1)}, bf16[2,6]{1,0:T(2,128)(2,1)}, u32[]{:S(2)}) copy-start(bf16[2,6]{1,0:T(2,128)(2,1)} %param.13) | copy-start | bytes 76
  7.2 71.3 %all-reduce.3.cloned.1.call-start = ((), (), s32[]{:S(2)}) async-start(), calls=%async_computation.2 | async-start | bytes 3604480 | tf_op jit(solution)/shard_map/psum | solution.py:94
  11.7 3.8 %copy-start.1 = (bf16[2,6,40,5632]{3,2,1,0:T(8,128)(2,1)}, bf16[2,6,40,5632]{3,2,1,0:T(8,128)(2,1)S(1)}, u32[]{:S(2)}) copy-start(bf16[2,6,40,5632]{3,2,1,0:T(8,128)(2,1)S(1)} %broadcast_select_fusion) | copy-start | bytes 16220164
  11.7 3.8 %copy-start.7 = (s32[40]{0:T(128)S(1)}, s32[40]{0:T(128)}, u32[]{:S(2)}) copy-start(s32[40]{0:T(128)} %param.10) | copy-start | bytes 484
  11.7 3.8 %copy-start.8 = (s32[256]{0:T(256)S(1)}, s32[256]{0:T(256)}, u32[]{:S(2)}) copy-start(s32[256]{0:T(256)} %param.11) | copy-start | bytes 3076
  15.6 28.0 %slice-start = ((s8[5406720]{0:T(1024)(128)(4,1)}), s8[4194304]{0:T(1024)(128)(4,1)S(1)}, s32[]{:S(2)}) async-start(s8[5406720]{0:T(1024)(128)(4,1)} %bitcast.62), calls=%async_computation.4 | async-start | bytes 8388608
  40.6 3.0 %slice-start.1 = ((s8[5406720]{0:T(1024)(128)(4,1)}), s8[1212416]{0:T(1024)(128)(4,1)S(1)}, s32[]{:S(2)}) async-start(s8[5406720]{0:T(1024)(128)(4,1)} %bitcast.62), calls=%async_computation.5 | async-start | bytes 2424832
  49.3 17.7 %copy-start.2 = (f32[16,2176]{1,0:T(8,128)S(1)}, f32[16,2176]{1,0:T(8,128)}, u32[]{:S(2)}) copy-start(f32[16,2176]{1,0:T(8,128)} %param.15) | copy-start | bytes 417796
  49.3 17.7 %copy-start.3 = (f32[16,2176]{1,0:T(8,128)S(1)}, f32[16,2176]{1,0:T(8,128)}, u32[]{:S(2)}) copy-start(f32[16,2176]{1,0:T(8,128)} %param.16) | copy-start | bytes 417796
  49.3 26.0 %copy-start.5 = (s32[40,11]{0,1:T(8,128)S(1)}, s32[40,11]{0,1:T(8,128)}, u32[]{:S(2)}) copy-start(s32[40,11]{0,1:T(8,128)} %param.14) | copy-start | bytes 5284
  50.4 41.9 %copy-start.6 = (s32[16,17]{1,0:T(8,128)S(1)}, s32[16,17]{1,0:T(8,128)}, u32[]{:S(2)}) copy-start(s32[16,17]{1,0:T(8,128)} %param.17) | copy-start | bytes 3268
  53.8 54.9 %all-to-all-start = ((bf16[64,2,1920]{2,1,0:T(2,128)(2,1)}), bf16[64,2,1920]{2,1,0:T(2,128)(2,1)S(1)}, u32[]{:S(2)}, u32[]{:S(2)}) async-start(bf16[64,2,1920]{2,1,0:T(2,128)(2,1)} %reshape.246), calls=%async_computation | async-start | bytes 983040 | tf_op jit(solution)/shard_map/all_to_all | solution.py:72
  67.0 83.6 %all-reduce.5.cloned.1.call-start = ((), (), s32[]{:S(2)}) async-start(), calls=%async_computation.3 | async-start | bytes 557056 | tf_op jit(solution)/shard_map/psum | solution.py:106
  67.7 52.6 %collective-permute-start.1 = (f32[2,1,2176]{2,1,0:T(1,128)}, f32[2,1,2176]{2,1,0:T(1,128)S(1)}, u32[]{:S(2)}, u32[]{:S(2)}) collective-permute-start(f32[2,1,2176]{2,1,0:T(1,128)} %get-tuple-element.17), channel_id=1, source_target_pairs={{0,1},{1,2},{2,3},{3,16},{16,17},{17,18},{18,19},{19,32},{32,33},{... | collective-permute-start | bytes 52232 | tf_op jit(solution)/shard_map/ppermute | solution.py:29
  71.9 48.4 %collective-permute-start = (f32[2,1,2176]{2,1,0:T(1,128)S(1)}, f32[2,1,2176]{2,1,0:T(1,128)S(1)}, u32[]{:S(2)}, u32[]{:S(2)}) collective-permute-start(f32[2,1,2176]{2,1,0:T(1,128)S(1)} %get-tuple-element.16), channel_id=1, source_target_pairs={{1,0},{2,1},{3,2},{16,3},{17,16},{18,17},{19,18},{32,19},{33,32},{... | collective-permute-start | bytes 52232 | tf_op jit(solution)/shard_map/ppermute | solution.py:31
  83.2 16.4 %collective-permute-start.3 = (f32[272,256]{1,0:T(8,128)S(1)}, f32[272,256]{1,0:T(8,128)S(1)}, u32[]{:S(2)}, u32[]{:S(2)}) collective-permute-start(f32[272,256]{1,0:T(8,128)S(1)} %get-tuple-element.9), channel_id=1, source_target_pairs={{1,0},{2,1},{3,2},{16,3},{17,16},{18,17},{19,18},{32,19},{33,32},{... | collective-permute-start | bytes 835592 | tf_op jit(solution)/shard_map/ppermute | solution.py:31
  89.5 18.1 %collective-permute-start.2 = (f32[272,256]{1,0:T(8,128)S(1)}, f32[272,256]{1,0:T(8,128)S(1)}, u32[]{:S(2)}, u32[]{:S(2)}) collective-permute-start(f32[272,256]{1,0:T(8,128)S(1)} %get-tuple-element.8), channel_id=1, source_target_pairs={{0,1},{1,2},{2,3},{3,16},{16,17},{17,18},{18,19},{19,32},{32,33},{... | collective-permute-start | bytes 835592 | tf_op jit(solution)/shard_map/ppermute | solution.py:29
  116.4 46.6 %all-to-all-start.1 = ((bf16[4,4,24,2560]{3,2,1,0:T(8,128)(2,1)}), bf16[4,4,24,2560]{3,2,1,0:T(8,128)(2,1)S(1)}, u32[]{:S(2)}, u32[]{:S(2)}) async-start(bf16[4,4,24,2560]{3,2,1,0:T(8,128)(2,1)} %stack.19), calls=%async_computation.1 | async-start | bytes 3932160 | tf_op jit(solution)/shard_map/all_to_all | solution.py:17
  152.6 18.7 %copy-start.4 = (f32[16,2176]{1,0:T(8,128)}, f32[16,2176]{1,0:T(8,128)S(1)}, u32[]{:S(2)}) copy-start(f32[16,2176]{1,0:T(8,128)S(1)} %get-tuple-element.11) | copy-start | bytes 417796
  152.6 16.0 %collective-permute-start.5 = (f32[16,2176]{1,0:T(8,128)S(1)}, f32[16,2176]{1,0:T(8,128)S(1)}, u32[]{:S(2)}, u32[]{:S(2)}) collective-permute-start(f32[16,2176]{1,0:T(8,128)S(1)} %get-tuple-element.11), channel_id=1, source_target_pairs={{1,0},{2,1},{3,2},{16,3},{17,16},{18,17},{19,18},{32,19},{33,32},{... | collective-permute-start | bytes 417800 | tf_op jit(solution)/shard_map/ppermute | solution.py:31
  161.0 10.2 %collective-permute-start.4 = (f32[16,2176]{1,0:T(8,128)S(1)}, f32[16,2176]{1,0:T(8,128)S(1)}, u32[]{:S(2)}, u32[]{:S(2)}) collective-permute-start(f32[16,2176]{1,0:T(8,128)S(1)} %get-tuple-element.11), channel_id=1, source_target_pairs={{0,1},{1,2},{2,3},{3,16},{16,17},{17,18},{18,19},{19,32},{32,33},{... | collective-permute-start | bytes 417800 | tf_op jit(solution)/shard_map/ppermute | solution.py:29
Sparse Core Ops, SparseCore 0:
  15.7 62.7 all-reduce.2
  108.7 41.8 all-reduce.4
